TPU v7x, 32 devices: a whole 2x2x4 slice. The times are simulated.
32 devices in a mesh: inp: 2 (over y), wt: 4 (over x, core), out: 4 (over z).
Axes of the slice: x: 2, y: 2, z: 4, core: 2. Of those that a mesh axis runs over, the one named last changes fastest.
Arguments:
- layer_input: bfloat16 [1280, 7168], P('inp', 'wt'), may hold values from -13.5 to 13.5
- w_qkv: bfloat16 [3, 7168, 4096], P(None, 'wt', ('inp', 'out')), may hold values from -0.0625 to 0.0625
- w_out: bfloat16 [4096, 7168], P(('inp', 'out'), 'wt'), may hold values from -0.09375 to 0.09375
- cotangent: bfloat16 [1280, 7168], P('inp', 'wt'), may hold values from -6 to 6
Outputs:
- grad_input: bfloat16 [1280, 7168], P('inp', ('wt', 'out'))
- grad_qkv: bfloat16 [3, 7168, 4096], P(None, 'wt', ('inp', 'out'))
- grad_out: bfloat16 [4096, 7168], P(('inp', 'out'), 'wt')
All inputs are finite; a program needn't handle non-finite values.
Results may differ from a plain program's by a relative error of at most 0.024.
Values may be sent and summed in bfloat16 or wider, within the bound.
A program may use at most 128 MiB of HBM per device.

v0:
```python
import math

import jax
import jax.numpy as jnp
from jax import lax
from jax.sharding import PartitionSpec as P

HEAD_DIM = 128


def attend_block(queries, key_rows, value_rows, grad_attended):
    length = queries.shape[0]
    scaling = 1.0 / math.sqrt(queries.shape[2])
    scores = (
        jnp.einsum("qhd,khd->hqk", queries, key_rows, preferred_element_type=jnp.float32) * scaling
    )
    row_index = jnp.arange(length)[:, None]
    col_index = jnp.arange(length)[None, :]
    causal = col_index <= row_index
    scores = jnp.where(causal[None], scores, -1e30)
    largest = jnp.max(scores, axis=2, keepdims=True)
    powers = jnp.exp(scores - largest)
    weights_f = powers / jnp.sum(powers, axis=2, keepdims=True)
    weights_b = weights_f.astype(jnp.bfloat16)
    attended = jnp.einsum(
        "hqk,khd->qhd", weights_b, value_rows, preferred_element_type=jnp.float32
    ).astype(jnp.bfloat16)
    grad_weights = jnp.einsum(
        "qhd,khd->hqk", grad_attended, value_rows, preferred_element_type=jnp.float32
    )
    row_dots = jnp.sum(grad_attended.astype(jnp.float32) * attended.astype(jnp.float32), axis=2)
    grad_scores = (
        weights_f * (grad_weights - jnp.transpose(row_dots)[:, :, None]) * scaling
    ).astype(jnp.bfloat16)
    grad_query = jnp.einsum(
        "hqk,khd->qhd", grad_scores, key_rows, preferred_element_type=jnp.float32
    ).astype(jnp.bfloat16)
    grad_key = jnp.einsum(
        "hqk,qhd->khd", grad_scores, queries, preferred_element_type=jnp.float32
    ).astype(jnp.bfloat16)
    grad_value = jnp.einsum(
        "hqk,qhd->khd", weights_b, grad_attended, preferred_element_type=jnp.float32
    ).astype(jnp.bfloat16)
    return (attended, grad_query, grad_key, grad_value)


def local(layer_input, w_qkv, w_out, cotangent):
    qkv_block, out_block = (
        lax.all_gather(w_qkv, "inp", axis=2, tiled=True),
        lax.all_gather(w_out, "inp", axis=0, tiled=True),
    )
    wt_count = lax.axis_size("wt")
    head_cols = out_block.shape[0] // wt_count
    local_heads = head_cols // HEAD_DIM
    length = layer_input.shape[0]
    qkv_part = jnp.einsum("td,cde->tce", layer_input, qkv_block, preferred_element_type=jnp.float32)
    grad_part = jnp.einsum("td,ed->te", cotangent, out_block, preferred_element_type=jnp.float32)
    qkv_mine, grad_mine = (
        lax.psum_scatter(qkv_part, "wt", scatter_dimension=2, tiled=True),
        lax.psum_scatter(grad_part, "wt", scatter_dimension=1, tiled=True),
    )
    projected = qkv_mine.astype(jnp.bfloat16)
    queries = projected[:, 0].reshape(length, local_heads, HEAD_DIM)
    key_rows = projected[:, 1].reshape(length, local_heads, HEAD_DIM)
    value_rows = projected[:, 2].reshape(length, local_heads, HEAD_DIM)
    grad_attn = grad_mine.astype(jnp.bfloat16).reshape(length, local_heads, HEAD_DIM)
    attended, grad_query, grad_key, grad_value = attend_block(
        queries, key_rows, value_rows, grad_attn
    )
    grad_rows = jnp.stack([grad_query, grad_key, grad_value], axis=1).reshape(length, 3, head_cols)
    attended_rows = attended.reshape(length, head_cols)
    grad_all, attended_all = (
        lax.all_gather(grad_rows, "wt", axis=2, tiled=True),
        lax.all_gather(attended_rows, "wt", axis=1, tiled=True),
    )
    partial_input = jnp.einsum(
        "tce,cde->td", grad_all, qkv_block, preferred_element_type=jnp.float32
    )
    grad_input = lax.psum_scatter(partial_input, "out", scatter_dimension=1, tiled=True).astype(
        jnp.bfloat16
    )
    qkv_term = jnp.einsum("td,tce->cde", layer_input, grad_all, preferred_element_type=jnp.float32)
    out_term = jnp.einsum("te,td->ed", attended_all, cotangent, preferred_element_type=jnp.float32)
    qkv_total = lax.psum_scatter(
        qkv_term.astype(jnp.bfloat16), "inp", scatter_dimension=2, tiled=True
    )
    out_total = lax.psum_scatter(
        out_term.astype(jnp.bfloat16), "inp", scatter_dimension=0, tiled=True
    )
    return (grad_input, qkv_total, out_total)


def solution(mesh):
    return jax.shard_map(
        local,
        mesh=mesh,
        in_specs=(
            P("inp", "wt"),
            P(None, "wt", ("inp", "out")),
            P(("inp", "out"), "wt"),
            P("inp", "wt"),
        ),
        out_specs=(P("inp", ("wt", "out")), P(None, "wt", ("inp", "out")), P(("inp", "out"), "wt")),
        check_vma=False,
    )
```

profile of v0, /device:TPU:0, one launch (start us, length us, event | category | flops | bytes accessed | tf_op | source)
XLA Modules:
  0.0 658.2 jit_solution(4052810943530010964)
XLA Ops:
  7.2 0.0 all-gather.7.cloned.1.call-start
  7.2 0.7 all-gather.7.cloned.1.call-update
  7.9 0.0 all-gather.5.cloned.1.call-start
  8.0 0.7 all-gather.5.cloned.1.call-update
  8.7 0.0 reduce-scatter.8.cloned.1.call-start
  8.7 54.4 %all-gather.7.cloned.1.call-done = bf16[1024,1792]{1,0:T(8,128)(2,1)} async-done(((bf16[512,1792]{1,0:T(8,128)(2,1)}), bf16[1024,1792]{1,0:T(8,128)(2,1)}) %all-gather.7.cloned.1.call-update) | async-done | bytes 3670032 | tf_op jit(solution)/shard_map/all_gather | solution.py:50
  63.1 6.8 %fusion.15 = f32[640,1024]{1,0:T(8,128)} fusion(bf16[640,1792]{1,0:T(8,128)(2,1)} %param.7, bf16[1024,1792]{1,0:T(8,128)(2,1)} %all-gather.7.cloned.1.call-done), kind=kOutput, calls=%fused_computation.28 | convolution fusion | flops 2348810240 | bytes 8585216 | tf_op jit(solution)/shard_map/td,ed->te/dot_general | solution.py:57
  69.9 0.0 reduce-scatter.8.cloned.1.call-update
  69.9 0.0 reduce-scatter.6.cloned.1.call-start
  70.0 130.0 %all-gather.5.cloned.1.call-done = bf16[3,1792,1024]{2,1,0:T(8,128)(2,1)} async-done(((bf16[3,1792,512]{2,1,0:T(8,128)(2,1)}), bf16[3,1792,1024]{2,1,0:T(8,128)(2,1)}) %all-gather.5.cloned.1.call-update) | async-done | bytes 11010064 | tf_op jit(solution)/shard_map/all_gather | solution.py:49
  200.0 12.0 %fusion.3 = f32[640,3,1024]{2,0,1:T(8,128)} fusion(bf16[3,1792,1024]{2,1,0:T(8,128)(2,1)} %all-gather.5.cloned.1.call-done, bf16[640,1792]{1,0:T(8,128)(2,1)S(1)} %copy-done), kind=kOutput, calls=%fused_computation.9 | convolution fusion | flops 7046430720 | bytes 21168128 | tf_op jit(solution)/shard_map/td,cde->tce/dot_general | solution.py:56
  212.0 0.0 all-gather.9.cloned.1.call-start
  212.0 0.9 iota_compare_fusion
  212.9 24.9 %reduce-scatter.8.cloned.1.call-done = f32[640,256]{1,0:T(8,128)} async-done(((f32[640,1024]{1,0:T(8,128)}), f32[640,256]{1,0:T(8,128)}) %reduce-scatter.8.cloned.1.call-update) | async-done | bytes 655376 | tf_op jit(solution)/shard_map/reduce_scatter | solution.py:60
  237.8 1.1 convert_element_type.55
  238.9 0.2 copy.34
  239.1 70.2 %reduce-scatter.6.cloned.1.call-done = f32[640,3,256]{2,0,1:T(8,128)} async-done(((f32[640,3,1024]{2,0,1:T(8,128)}), f32[640,3,256]{2,0,1:T(8,128)}) %reduce-scatter.6.cloned.1.call-update) | async-done | bytes 1966096 | tf_op jit(solution)/shard_map/reduce_scatter | solution.py:59
  309.4 1.6 convert_element_type.54
  311.0 0.8 fusion.13
  311.8 0.9 copy.35
  312.7 0.2 copy.33
  312.9 1.2 copy.32
  314.1 4.1 fusion.14
  318.2 2.2 fusion.8
  320.5 1.4 convolution_convert_fusion.1
  321.8 1.2 multiply_reduce_fusion
  323.1 0.8 multiply_convert_fusion
  323.9 1.4 convolution_convert_fusion.2
  325.2 0.5 convolution_convert_fusion.3
  325.7 0.2 copy.21
  325.9 1.1 copy.22
  327.0 0.9 copy.23
  328.0 2.0 pad_maximum_fusion
  330.0 0.0 all-gather.11.cloned.1.call-start
  330.0 0.5 all-gather.11.cloned.1.call-update
  330.6 0.2 reduce-scatter.10.cloned.1.call-start
  330.8 32.9 %all-gather.9.cloned.1.call-done = bf16[640,3,1024]{2,0,1:T(8,128)(2,1)} async-done(((bf16[640,3,256]{2,0,1:T(8,128)(2,1)}), bf16[640,3,1024]{2,0,1:T(8,128)(2,1)}) %all-gather.9.cloned.1.call-update) | async-done | bytes 3932176 | tf_op jit(solution)/shard_map/all_gather | solution.py:73
  363.7 14.1 %convolution_bitcast_fusion = f32[640,1792]{0,1:T(8,128)} fusion(bf16[640,3,1024]{2,0,1:T(8,128)(2,1)} %all-gather.9.cloned.1.call-done, bf16[3,1792,1024]{2,1,0:T(8,128)(2,1)} %all-gather.5.cloned.1.call-done), kind=kOutput, calls=%fused_computation.3 | convolution fusion | flops 7046430720 | bytes 19529728 | tf_op jit(solution)/shard_map/tce,cde->td/dot_general | solution.py:76
  377.7 0.0 reduce-scatter.12.cloned.1.call-start
  377.8 14.6 %convert_bitcast_fusion = bf16[3,1792,1024]{1,2,0:T(8,128)(2,1)} fusion(bf16[640,3,1024]{2,0,1:T(8,128)(2,1)} %all-gather.9.cloned.1.call-done, bf16[640,1792]{1,0:T(8,128)(2,1)S(1)} %copy-done), kind=kOutput, calls=%fused_computation.1 | convolution fusion | flops 7051935744 | bytes 17235968 | tf_op jit(solution)/shard_map/td,tce->cde/dot_general | solution.py:82
  392.4 0.0 reduce-scatter.14.cloned.1.call-start
  392.4 0.0 all-gather.11.cloned.1.call-done
  392.4 7.1 %convolution_convert_fusion = bf16[1024,1792]{1,0:T(8,128)(2,1)} fusion(bf16[640,1024]{0,1:T(8,128)(2,1)} %all-gather.11.cloned.1.call-done, bf16[640,1792]{1,0:T(8,128)(2,1)} %param.7), kind=kOutput, calls=%fused_computation.2 | convolution fusion | flops 2350645248 | bytes 7274496 | tf_op jit(solution)/shard_map/te,td->ed/dot_general | solution.py:83
  399.5 69.8 %reduce-scatter.10.cloned.1.call-done = f32[640,448]{0,1:T(8,128)} async-done(((f32[640,1792]{0,1:T(8,128)}), f32[640,448]{0,1:T(8,128)}) %reduce-scatter.10.cloned.1.call-update) | async-done | bytes 1146896 | tf_op jit(solution)/shard_map/reduce_scatter | solution.py:79
  469.3 2.1 convert_element_type.68
  471.5 128.3 %reduce-scatter.12.cloned.1.call-done = bf16[3,1792,512]{1,2,0:T(8,128)(2,1)} async-done(((bf16[3,1792,1024]{1,2,0:T(8,128)(2,1)}), bf16[3,1792,512]{1,2,0:T(8,128)(2,1)}) %reduce-scatter.12.cloned.1.call-update) | async-done | bytes 5505040 | tf_op jit(solution)/shard_map/reduce_scatter | solution.py:84
  599.7 8.3 %copy.25 = bf16[3,1792,512]{2,1,0:T(8,128)(2,1)} copy(bf16[3,1792,512]{1,2,0:T(8,128)(2,1)} %reduce-scatter.12.cloned.1.call-done) | data formatting | bytes 11010048
  608.0 43.7 %reduce-scatter.14.cloned.1.call-done = bf16[512,1792]{1,0:T(8,128)(2,1)} async-done(((bf16[1024,1792]{1,0:T(8,128)(2,1)}), bf16[512,1792]{1,0:T(8,128)(2,1)}) %reduce-scatter.14.cloned.1.call-update) | async-done | bytes 1835024 | tf_op jit(solution)/shard_map/reduce_scatter | solution.py:87
  (13 shorter events, 0.1 us)
Async XLA Ops:
  7.2 192.8 %copy-start = (bf16[640,1792]{1,0:T(8,128)(2,1)S(1)}, bf16[640,1792]{1,0:T(8,128)(2,1)}, u32[]{:S(2)}) copy-start(bf16[640,1792]{1,0:T(8,128)(2,1)} %param.4) | copy-start | bytes 6881284
  7.2 56.0 %all-gather.7.cloned.1.call-start = ((), (), s32[]{:S(2)}) async-start(), calls=%async_computation.7 | async-start | bytes 5505024 | tf_op jit(solution)/shard_map/all_gather | solution.py:50
  7.9 192.1 %all-gather.5.cloned.1.call-start = ((), (), s32[]{:S(2)}) async-start(), calls=%async_computation.5 | async-start | bytes 16515072 | tf_op jit(solution)/shard_map/all_gather | solution.py:49
  8.7 229.2 %reduce-scatter.8.cloned.1.call-start = ((), (), s32[]{:S(2)}) async-start(), calls=%async_computation.8 | async-start | bytes 3276800 | tf_op jit(solution)/shard_map/reduce_scatter | solution.py:60
  69.9 239.5 %reduce-scatter.6.cloned.1.call-start = ((), (), s32[]{:S(2)}) async-start(), calls=%async_computation.6 | async-start | bytes 9830400 | tf_op jit(solution)/shard_map/reduce_scatter | solution.py:59
  212.0 151.7 %all-gather.9.cloned.1.call-start = ((), (), s32[]{:S(2)}) async-start(), calls=%async_computation.9 | async-start | bytes 4915200 | tf_op jit(solution)/shard_map/all_gather | solution.py:73
  318.2 3.6 copy-start.3
  320.5 2.6 copy-start.1
  323.8 3.2 copy-start.2
  330.0 62.4 %all-gather.11.cloned.1.call-start = ((), (), s32[]{:S(2)}) async-start(), calls=%async_computation.12 | async-start | bytes 1638400 | tf_op jit(solution)/shard_map/all_gather | solution.py:74
  330.6 138.8 %reduce-scatter.10.cloned.1.call-start = ((), (), s32[]{:S(2)}) async-start(), calls=%async_computation.10 | async-start | bytes 5734400 | tf_op jit(solution)/shard_map/reduce_scatter | solution.py:79
  377.7 222.0 %reduce-scatter.12.cloned.1.call-start = ((), (), s32[]{:S(2)}) async-start(), calls=%async_computation.11 | async-start | bytes 16515072 | tf_op jit(solution)/shard_map/reduce_scatter | solution.py:84
  392.4 259.3 %reduce-scatter.14.cloned.1.call-start = ((), (), s32[]{:S(2)}) async-start(), calls=%async_computation.13 | async-start | bytes 5505024 | tf_op jit(solution)/shard_map/reduce_scatter | solution.py:87
Sparse Core Ops, SparseCore 0:
  9.6 53.5 all-gather.6
  64.7 135.2 all-gather.4
  203.1 34.6 reduce-scatter.7
  240.4 68.9 reduce-scatter.5
  330.1 33.4 all-gather.8
  365.1 18.1 all-gather.10
  386.2 83.1 reduce-scatter.9
  471.6 128.0 reduce-scatter.11
  602.6 49.0 reduce-scatter.13
where the time goes:
time: 659 us; the launch traced here: 658 us
  waiting for transfers between devices  556 us (84%)
  matrix products  63.7 us (10%)
  between operations  13.9 us (2%)
  local copies, waits for them, and re-layouts  13.8 us (2%)
  other arithmetic  10 us (2%)
    all_gather x1, waiting for transfers between devices, local(): lax.all_gather(w_qkv, 'inp', axis=2, tiled=True)  130 us
    reduce_scatter x1, waiting for transfers between devices, local(): lax.psum_scatter(qkv_term.astype(jnp.bfloat16), 'inp', scatter_dimension=...  128 us
    reduce_scatter x1, waiting for transfers between devices, local(): lax.psum_scatter(qkv_part, 'wt', scatter_dimension=2, tiled=True)  70.2 us
    reduce_scatter x1, waiting for transfers between devices, local(): lax.psum_scatter(partial_input, 'out', scatter_dimension=1, tiled=True)  69.8 us
    all_gather x1, waiting for transfers between devices, local(): lax.all_gather(w_out, 'inp', axis=0, tiled=True)  54.4 us
    reduce_scatter x1, waiting for transfers between devices, local(): lax.psum_scatter(out_term.astype(jnp.bfloat16), 'inp', scatter_dimension=...  43.7 us
    all_gather x1, waiting for transfers between devices, local(): lax.all_gather(grad_rows, 'wt', axis=2, tiled=True)  32.9 us
    reduce_scatter x1, waiting for transfers between devices, local(): lax.psum_scatter(grad_part, 'wt', scatter_dimension=1, tiled=True)  24.9 us
  transfers between devices with their start and end apart: 9, of which 8 were waited for; matrix products, arithmetic and copies ran while one was open for 10% of the time, Pallas kernels for 0%

commit v1 on v0

--- a/solution.py
+++ b/solution.py
@@ -3,6 +3,8 @@
 import jax
 import jax.numpy as jnp
 from jax import lax
+from jax.experimental import pallas as pl
+from jax.experimental.pallas import tpu as pltpu
 from jax.sharding import PartitionSpec as P
 
 HEAD_DIM = 128
@@ -90,9 +92,327 @@
     return (grad_input, qkv_total, out_total)
 
 
+BF = jnp.bfloat16
+F32 = jnp.float32
+N = HEAD_DIM
+MESH = pl.DeviceIdType.MESH
+
+
+def dot(a, b, dims):
+    return lax.dot_general(a, b, (dims, ((), ())), preferred_element_type=F32)
+
+
+def kernel(
+    x_ref, w_ref, wo_ref, c_ref, gi_ref, gw_ref, go_ref,
+    xo, co, part, from_core, from_x, mine, grads, att_t, gin, from_pair, from_cross,
+    own_sum, far_sum, from_inp, acc_k, acc_v, send, recv,
+):
+    inp = lax.axis_index("inp")
+    wt = lax.axis_index("wt")
+    z = lax.axis_index("out")
+    x_at, core = wt // 2, wt % 2
+    length = x_ref.shape[0]
+    width = x_ref.shape[1]
+    cols = w_ref.shape[2]
+    quarter = width // 4
+    half = length // 2
+    chunk = half // 2
+    parity = z % 2
+    z_pair, z_cross, z_far = z + 1 - 2 * parity, (z + 2) % 4, 3 - z
+    inp_peer = {"inp": 1 - inp}
+    core_peer = {"wt": wt + 1 - 2 * core}
+    x_peer = {"wt": (wt + 2) % 4}
+    pair_peer = {"out": z_pair}
+    cross_peer = {"out": z_cross}
+
+    barrier = pltpu.get_barrier_semaphore()
+    for peer in (inp_peer, core_peer, x_peer, pair_peer, cross_peer):
+        pl.semaphore_signal(barrier, inc=1, device_id=peer, device_id_type=MESH)
+    pl.semaphore_wait(barrier, 5)
+
+    used = [0]
+
+    def copy(src, dst, peer):
+        k = used[0]
+        used[0] += 1
+        return pltpu.make_async_remote_copy(
+            src_ref=src, dst_ref=dst, send_sem=send.at[k], recv_sem=recv.at[k],
+            device_id=peer, device_id_type=MESH,
+        )
+
+    def head(x, c):
+        return pl.ds(pl.multiple_of((2 * x + c) * N, N), N)
+
+    fetch, share = [], []
+    for here, there in ((c_ref, co), (x_ref, xo)):
+        for k in range(2):
+            rows = pl.ds(pl.multiple_of(parity * half + k * chunk, 32), chunk)
+            fetch.append(copy(here.at[rows], there.at[rows], inp_peer))
+            share.append(copy(there.at[rows], there.at[rows], pair_peer))
+
+    def forward(k):
+        fetch[k].wait()
+        share[k].start()
+        if k + 2 < 4:
+            fetch[k + 2].start()
+
+    def project_out(acts):
+        @pl.loop(0, 4)
+        def _(t):
+            rows = pl.ds(pl.multiple_of((t // 2) * half, half), half)
+            n = cols // 2
+            at = pl.ds(pl.multiple_of((t % 2) * n, n), n)
+            part[3, rows, at] = dot(acts[rows, :], wo_ref[at, :], ((1,), (1,))).astype(BF)
+
+    def project_in(acts):
+        @pl.loop(0, 12)
+        def _(t):
+            rows = pl.ds(pl.multiple_of((t % 2) * half, half), half)
+            n = cols // 2
+            at = pl.ds(pl.multiple_of(((t // 2) % 2) * n, n), n)
+            c = t // 4
+            part[c, rows, at] = dot(acts[rows, :], w_ref[c, :, at], ((1,), (0,))).astype(BF)
+
+    class Sequence:
+        pass
+
+    seqs = []
+    for s in range(2):
+        q = Sequence()
+        q.core = [
+            copy(part.at[:, :, head(x, 1 - core)], from_core.at[s, k], core_peer)
+            for k, x in ((0, 1 - x_at), (1, x_at))
+        ]
+        q.across = copy(part.at[:, :, head(1 - x_at, core)], from_x.at[s], x_peer)
+        own = grads.at[s, :, :, head(x_at, core)]
+        other = grads.at[s, :, :, head(1 - x_at, core)]
+        q.give_x = copy(own, own, x_peer)
+        q.give_core = copy(own, own, core_peer)
+        q.give_other = copy(other, other, core_peer)
+        q.pair, q.cross = [], []
+        for r in range(2):
+            rows = pl.ds(r * half, half)
+            q.pair.append(
+                (
+                    copy(gin.at[s, z_far, rows], from_pair.at[s, 0, rows], pair_peer),
+                    copy(gin.at[s, z_pair, rows], from_pair.at[s, 1, rows], pair_peer),
+                )
+            )
+            q.cross.append(copy(gin.at[s, z_cross, rows], from_cross.at[s, rows], cross_peer))
+        seqs.append(q)
+    back = [
+        copy(far_sum.at[pl.ds(r * half, half)], from_inp.at[pl.ds(r * half, half)], inp_peer)
+        for r in range(2)
+    ]
+
+    def scatter_start(s):
+        for c in seqs[s].core:
+            c.start()
+
+    def scatter_across(s):
+        for c in seqs[s].core:
+            c.wait()
+        at = head(1 - x_at, core)
+        for j in range(4):
+            total = part[j, :, at].astype(F32) + from_core[s, 0, j].astype(F32)
+            part[j, :, at] = total.astype(BF)
+        seqs[s].across.start()
+
+    def scatter_end(s):
+        at = head(x_at, core)
+        seqs[s].across.wait()
+        for j in range(4):
+            total = part[j, :, at].astype(F32) + from_core[s, 1, j].astype(F32)
+            mine[j] = (total + from_x[s, j].astype(F32)).astype(BF)
+
+    def attention(s):
+        scaling = 1.0 / math.sqrt(N)
+        at = head(x_at, core)
+        acc_k[...] = jnp.zeros_like(acc_k)
+        acc_v[...] = jnp.zeros_like(acc_v)
+
+        @pl.loop(0, length // N)
+        def _(b):
+            rows = pl.ds(pl.multiple_of(b * N, N), N)
+            queries, grad = mine[0, rows, :], mine[3, rows, :]
+            keys, values = mine[1], mine[2]
+            scores = dot(queries, keys, ((1,), (1,))) * scaling
+            row = lax.broadcasted_iota(jnp.int32, (N, length), 0) + b * N
+            col = lax.broadcasted_iota(jnp.int32, (N, length), 1)
+            scores = jnp.where(col <= row, scores, -1e30)
+            powers = jnp.exp(scores - jnp.max(scores, axis=1, keepdims=True))
+            probs = powers / jnp.sum(powers, axis=1, keepdims=True)
+            probs_b = probs.astype(BF)
+            attended = dot(probs_b, values, ((1,), (0,))).astype(BF)
+            grad_probs = dot(grad, values, ((1,), (1,)))
+            dots = jnp.sum(grad.astype(F32) * attended.astype(F32), axis=1, keepdims=True)
+            grad_scores = (probs * (grad_probs - dots) * scaling).astype(BF)
+            grads[s, 0, rows, at] = dot(grad_scores, keys, ((1,), (0,))).astype(BF)
+            grads[s, 3, rows, at] = attended
+            acc_k[...] += dot(grad_scores, queries, ((0,), (0,)))
+            acc_v[...] += dot(probs_b, grad, ((0,), (0,)))
+
+        grads[s, 1, :, at] = acc_k[...].astype(BF)
+        grads[s, 2, :, at] = acc_v[...].astype(BF)
+
+    def gather_start(s):
+        seqs[s].give_x.start()
+        seqs[s].give_core.start()
+
+    def gather_pass(s):
+        seqs[s].give_x.wait()
+        seqs[s].give_other.start()
+
+    def gather_end(s):
+        seqs[s].give_core.wait()
+        seqs[s].give_other.wait()
+
+    def input_rows(s, r):
+        rows = pl.ds(r * half, half)
+
+        @pl.loop(0, 4)
+        def _(k):
+            at = pl.ds(pl.multiple_of(k * quarter, 64), quarter)
+            total = dot(grads[s, 0, rows, :], w_ref[0, at, :], ((1,), (1,)))
+            for c in (1, 2):
+                total = total + dot(grads[s, c, rows, :], w_ref[c, at, :], ((1,), (1,)))
+            gin[s, k, rows, :] = total.astype(BF)
+
+        for c in seqs[s].pair[r]:
+            c.start()
+
+    def input_cross(s, r):
+        rows = pl.ds(r * half, half)
+        for c in seqs[s].pair[r]:
+            c.wait()
+        total = gin[s, z_cross, rows, :].astype(F32) + from_pair[s, 0, rows, :].astype(F32)
+        gin[s, z_cross, rows, :] = total.astype(BF)
+        seqs[s].cross[r].start()
+
+    def input_end(s, r, out):
+        rows = pl.ds(r * half, half)
+        seqs[s].cross[r].wait()
+        total = gin[s, z, rows, :].astype(F32) + from_pair[s, 1, rows, :].astype(F32)
+        out[rows, :] = (total + from_cross[s, rows, :].astype(F32)).astype(out.dtype)
+
+    def weight_in(s, acts):
+        @pl.loop(0, width // 256)
+        def _(m):
+            at = pl.ds(pl.multiple_of(m * 256, 256), 256)
+            turned = acts[:, at].T
+            for c in range(3):
+                term = dot(turned, grads[s, c], ((1,), (0,))).astype(BF)
+                if s == 1:
+                    term = (term.astype(F32) + gw_ref[c, at, :].astype(F32)).astype(BF)
+                gw_ref[c, at, :] = term
+
+    def weight_out(s, cots):
+        att_t[...] = grads[s, 3].T
+
+        @pl.loop(0, width // 256)
+        def _(m):
+            at = pl.ds(pl.multiple_of(m * 256, 256), 256)
+            term = dot(att_t[...], cots[:, at], ((1,), (0,))).astype(BF)
+            if s == 1:
+                term = (term.astype(F32) + go_ref[:, at].astype(F32)).astype(BF)
+            go_ref[:, at] = term
+
+    fetch[0].start()
+    fetch[1].start()
+    project_out(c_ref)
+    forward(0)
+    project_in(x_ref)
+    scatter_start(0)
+    forward(1)
+    scatter_across(0)
+    scatter_end(0)
+    attention(0)
+    gather_start(0)
+    forward(2)
+    share[0].wait()
+    share[1].wait()
+    project_out(co)
+    gather_pass(0)
+    forward(3)
+    gather_end(0)
+    input_rows(0, 0)
+    input_rows(0, 1)
+    share[2].wait()
+    share[3].wait()
+    project_in(xo)
+    scatter_start(1)
+    weight_out(0, c_ref)
+    scatter_across(1)
+    weight_in(0, x_ref)
+    input_cross(0, 0)
+    input_cross(0, 1)
+    scatter_end(1)
+    attention(1)
+    gather_start(1)
+    input_end(0, 0, own_sum)
+    input_end(0, 1, own_sum)
+    gather_pass(1)
+    gather_end(1)
+    input_rows(1, 0)
+    input_rows(1, 1)
+    weight_out(1, co)
+    input_cross(1, 0)
+    weight_in(1, xo)
+    input_cross(1, 1)
+    for r in range(2):
+        input_end(1, r, far_sum)
+        back[r].start()
+    for r in range(2):
+        rows = pl.ds(r * half, half)
+        back[r].wait()
+        gi_ref[rows, :] = (own_sum[rows, :] + from_inp[rows, :].astype(F32)).astype(BF)
+
+
+def local_fast(layer_input, w_qkv, w_out, cotangent):
+    length, width = layer_input.shape
+    cols = w_qkv.shape[2]
+    quarter = width // 4
+    vmem = pl.BlockSpec(memory_space=pltpu.VMEM)
+    return pl.pallas_call(
+        kernel,
+        out_shape=[
+            jax.ShapeDtypeStruct((length, quarter), BF),
+            jax.ShapeDtypeStruct(w_qkv.shape, BF),
+            jax.ShapeDtypeStruct(w_out.shape, BF),
+        ],
+        in_specs=[vmem] * 4,
+        out_specs=[vmem] * 3,
+        scratch_shapes=[
+            pltpu.VMEM((length, width), BF),
+            pltpu.VMEM((length, width), BF),
+            pltpu.VMEM((4, length, cols), BF),
+            pltpu.VMEM((2, 2, 4, length, N), BF),
+            pltpu.VMEM((2, 4, length, N), BF),
+            pltpu.VMEM((4, length, N), BF),
+            pltpu.VMEM((2, 4, length, cols), BF),
+            pltpu.VMEM((cols, length), BF),
+            pltpu.VMEM((2, 4, length, quarter), BF),
+            pltpu.VMEM((2, 2, length, quarter), BF),
+            pltpu.VMEM((2, length, quarter), BF),
+            pltpu.VMEM((length, quarter), F32),
+            pltpu.VMEM((length, quarter), BF),
+            pltpu.VMEM((length, quarter), BF),
+            pltpu.VMEM((length, N), F32),
+            pltpu.VMEM((length, N), F32),
+            pltpu.SemaphoreType.DMA((40,)),
+            pltpu.SemaphoreType.DMA((40,)),
+        ],
+        compiler_params=pltpu.CompilerParams(
+            collective_id=0, has_side_effects=True, vmem_limit_bytes=62 * 2**20
+        ),
+    )(layer_input, w_qkv, w_out, cotangent)
+
+
 def solution(mesh):
+    sizes = dict(mesh.shape)
+    fits = sizes["inp"] == 2 and sizes["wt"] == 4 and sizes["out"] == 4
     return jax.shard_map(
-        local,
+        local_fast if fits else local,
         mesh=mesh,
         in_specs=(
             P("inp", "wt"),

time: 659 us -> 211 us (0.32)
  waiting for transfers between devices: 556 us -> 0 us
  Pallas kernels: 0 us -> 201 us
  matrix products: 63.7 us -> 0 us
  between operations: 13.9 us -> 0.64 us
  other arithmetic: 10 us -> 0 us
    reduce_scatter x5 -> x0, waiting for transfers between devices: 337 us -> none  [the longest x1 128 us: local(): lax.psum_scatter(qkv_term.astype(jnp.bfloat16), 'inp', scatter_dimension=...]
    all_gather x4 -> x0, waiting for transfers between devices: 217 us -> none  [the longest x1 130 us: local(): lax.all_gather(w_qkv, 'inp', axis=2, tiled=True)]
    pallas_call x0 -> x1, Pallas kernels: none -> 201 us  [local_fast(): pl.pallas_call(kernel, out_shape=[jax.ShapeDtypeStruct((length, quarter),...]
    dot_general x10 -> x0, matrix products: 59.6 us -> none  [the longest x1 14.6 us: local(): jnp.einsum('td,tce->cde', layer_input, grad_all, preferred_element_type=j...]
    convert_element_type x4 -> x0, other arithmetic: 7.12 us -> none  [the longest x1 2.23 us: attend_block(): weights_b = weights_f.astype(jnp.bfloat16)]
  transfers between devices with their start and end apart: 9 -> 0, of which waited for: 8 -> 0; matrix products, arithmetic and copies ran while one was open for 10% -> 0% of each run, Pallas kernels for 0% -> 0%
where the time goes in v1:
time: 211 us; the launch traced here: 210 us
  Pallas kernels  201 us (95%)
  local copies, waits for them, and re-layouts  8.88 us (4%)
    pallas_call x1, Pallas kernels, local_fast(): pl.pallas_call(kernel, out_shape=[jax.ShapeDtypeStruct((length, quarter),...  201 us
    unnamed x4, local copies, waits for them, and re-layouts  6.72 us

profile of v1, /device:TPU:0, one launch (start us, length us, event | category | flops | bytes accessed | tf_op | source)
XLA Modules:
  0.0 210.5 jit_solution(12050914368178669056)
XLA Ops:
  0.6 201.0 %shard_map.67 = (bf16[640,448]{1,0:T(8,128)(2,1)}, bf16[3,1792,512]{2,1,0:T(8,128)(2,1)}, bf16[512,1792]{1,0:T(8,128)(2,1)}) custom-call(bf16[640,1792]{1,0:T(8,128)(2,1)} %x_ref.1, bf16[3,1792,512]{2,1,0:T(8,128)(2,1)} %w_ref.1, bf16[512,1792]{1,0:T(8,128)(2,1)} %wo_ref.1, bf16[640,1792]{1,0:T(8,128)(2,1)} %c_ref.1), custom_call_target="tpu_custom_call" | custom-call | tf_op jit(solution)/shard_map/pallas_call | solution.py:376
  201.6 2.2 %copy.7 = bf16[640,448]{0,1:T(8,128)(2,1)} copy(bf16[640,448]{1,0:T(8,128)(2,1)} %get-tuple-element.3) | data formatting | bytes 1146880 | tf_op jit(solution)/shard_map/pallas_call | solution.py:376
  203.7 0.0 copy-start
  203.7 5.5 %copy.10 = bf16[3,1792,512]{2,1,0:T(8,128)(2,1)} copy(bf16[3,1792,512]{2,1,0:T(8,128)(2,1)} %get-tuple-element.10) | data formatting | bytes 11010048
  209.2 0.0 copy-done
  209.2 1.2 copy.11
Async XLA Ops:
  203.7 5.5 %copy-start = (bf16[512,1792]{1,0:T(8,128)(2,1)S(1)}, bf16[512,1792]{1,0:T(8,128)(2,1)}, u32[]{:S(2)}) copy-start(bf16[512,1792]{1,0:T(8,128)(2,1)} %get-tuple-element.11) | copy-start | bytes 5505028

commit v2 on v1

--- a/solution.py
+++ b/solution.py
@@ -267,30 +267,28 @@
         seqs[s].give_core.wait()
         seqs[s].give_other.wait()
 
-    def input_rows(s, r):
-        rows = pl.ds(r * half, half)
-
-        @pl.loop(0, 4)
-        def _(k):
+    def input_all(s):
+        for order, k in enumerate((z_far, z_cross, z_pair, z)):
             at = pl.ds(pl.multiple_of(k * quarter, 64), quarter)
-            total = dot(grads[s, 0, rows, :], w_ref[0, at, :], ((1,), (1,)))
-            for c in (1, 2):
-                total = total + dot(grads[s, c, rows, :], w_ref[c, at, :], ((1,), (1,)))
-            gin[s, k, rows, :] = total.astype(BF)
-
-        for c in seqs[s].pair[r]:
-            c.start()
+            for r in range(2):
+                rows = pl.ds(r * half, half)
+                total = dot(grads[s, 0, rows, :], w_ref[0, at, :], ((1,), (1,)))
+                for c in (1, 2):
+                    total = total + dot(grads[s, c, rows, :], w_ref[c, at, :], ((1,), (1,)))
+                gin[s, k, rows, :] = total.astype(BF)
+                if order % 2 == 0:
+                    seqs[s].pair[r][order // 2].start()
 
     def input_cross(s, r):
         rows = pl.ds(r * half, half)
-        for c in seqs[s].pair[r]:
-            c.wait()
+        seqs[s].pair[r][0].wait()
         total = gin[s, z_cross, rows, :].astype(F32) + from_pair[s, 0, rows, :].astype(F32)
         gin[s, z_cross, rows, :] = total.astype(BF)
         seqs[s].cross[r].start()
 
     def input_end(s, r, out):
         rows = pl.ds(r * half, half)
+        seqs[s].pair[r][1].wait()
         seqs[s].cross[r].wait()
         total = gin[s, z, rows, :].astype(F32) + from_pair[s, 1, rows, :].astype(F32)
         out[rows, :] = (total + from_cross[s, rows, :].astype(F32)).astype(out.dtype)
@@ -335,13 +333,12 @@
     gather_pass(0)
     forward(3)
     gather_end(0)
-    input_rows(0, 0)
-    input_rows(0, 1)
+    weight_out(0, c_ref)
     share[2].wait()
     share[3].wait()
     project_in(xo)
     scatter_start(1)
-    weight_out(0, c_ref)
+    input_all(0)
     scatter_across(1)
     weight_in(0, x_ref)
     input_cross(0, 0)
@@ -353,12 +350,11 @@
     input_end(0, 1, own_sum)
     gather_pass(1)
     gather_end(1)
-    input_rows(1, 0)
-    input_rows(1, 1)
+    input_all(1)
+    input_cross(1, 0)
     weight_out(1, co)
-    input_cross(1, 0)
+    input_cross(1, 1)
     weight_in(1, xo)
-    input_cross(1, 1)
     for r in range(2):
         input_end(1, r, far_sum)
         back[r].start()

time: 211 us -> 207 us (0.981)
  Pallas kernels: 201 us -> 197 us
    pallas_call x1, Pallas kernels: 201 us -> 197 us  [local_fast(): pl.pallas_call(kernel, out_shape=[jax.ShapeDtypeStruct((length, quarter),...]
where the time goes in v2:
time: 207 us
  Pallas kernels  197 us (95%)
  local copies, waits for them, and re-layouts  8.88 us (4%)
    pallas_call x1, Pallas kernels, local_fast(): pl.pallas_call(kernel, out_shape=[jax.ShapeDtypeStruct((length, quarter),...  197 us
    unnamed x4, local copies, waits for them, and re-layouts  6.72 us

profile of v2, /device:TPU:0, one launch (start us, length us, event | category | flops | bytes accessed | tf_op | source)
XLA Modules:
  0.0 206.5 jit_solution(139227253238165089)
XLA Ops:
  0.6 197.0 %shard_map.67 = (bf16[640,448]{1,0:T(8,128)(2,1)}, bf16[3,1792,512]{2,1,0:T(8,128)(2,1)}, bf16[512,1792]{1,0:T(8,128)(2,1)}) custom-call(bf16[640,1792]{1,0:T(8,128)(2,1)} %x_ref.1, bf16[3,1792,512]{2,1,0:T(8,128)(2,1)} %w_ref.1, bf16[512,1792]{1,0:T(8,128)(2,1)} %wo_ref.1, bf16[640,1792]{1,0:T(8,128)(2,1)} %c_ref.1), custom_call_target="tpu_custom_call" | custom-call | tf_op jit(solution)/shard_map/pallas_call | solution.py:372
  197.6 2.2 %copy.7 = bf16[640,448]{0,1:T(8,128)(2,1)} copy(bf16[640,448]{1,0:T(8,128)(2,1)} %get-tuple-element.3) | data formatting | bytes 1146880 | tf_op jit(solution)/shard_map/pallas_call | solution.py:372
  199.8 0.0 copy-start
  199.8 5.5 %copy.10 = bf16[3,1792,512]{2,1,0:T(8,128)(2,1)} copy(bf16[3,1792,512]{2,1,0:T(8,128)(2,1)} %get-tuple-element.10) | data formatting | bytes 11010048
  205.3 0.0 copy-done
  205.3 1.2 copy.11
Async XLA Ops:
  199.8 5.5 %copy-start = (bf16[512,1792]{1,0:T(8,128)(2,1)S(1)}, bf16[512,1792]{1,0:T(8,128)(2,1)}, u32[]{:S(2)}) copy-start(bf16[512,1792]{1,0:T(8,128)(2,1)} %get-tuple-element.11) | copy-start | bytes 5505028
